TPU v7x, 256 devices: a whole 4x4x8 slice. The times are simulated.
256 devices in a mesh: layer: 4 (over x), row: 8 (over z), col: 8 (over y, core).
Axes of the slice: x: 4, y: 4, z: 8, core: 2. Of those that a mesh axis runs over, the one named last changes fastest.
Arguments:
- a_values: bfloat16 [8, 32, 24, 128, 128], P('row', ('layer', 'col')), may hold values from -6 to 6
- a_rows: int32 [8, 32, 24], P('row', ('layer', 'col')), may hold values from 0 to 3, as said below
- a_ks: int32 [8, 32, 24], P('row', ('layer', 'col')), may hold values from 0 to 31
- a_count: int32 [32, 8], P(('layer', 'col'), 'row'), may hold values from 1 to 24, 64 in all within a row
- t_panel: bfloat16 [131072, 2048], P(('layer', 'col'), 'row'), may hold values from -0.0625 to 0.0625
Outputs:
- next_sign: bfloat16 [4096, 2048], P(('layer', 'col'), 'row')
Inputs may be any that keep to these rules, and one draw needn't show every extreme that they name: Within one device's 24 slots the pairs (a_rows, a_ks) are all different. `a_count`: for every inner panel the 8 counts sum to exactly 64, and one of them is exactly 24.
All inputs are finite; a program needn't handle non-finite values. No bound on the sum of `a_count` on one device may be relied on, other than what follows from the above.
Results may differ from a plain program's by a relative error of at most 0.001.
Values may be sent and summed in bfloat16 or wider, within the bound.
A program may use at most 128 MiB of HBM per device.

v0:
```python
import jax
import jax.numpy as jnp
from jax import lax
from jax.sharding import PartitionSpec as P

RB = 4


def live_values(block_values, counts):
    is_live = lax.broadcasted_iota(jnp.int32, block_values.shape[:2], 1) < counts[:, None]
    return jnp.where(is_live[:, :, None, None], block_values, jnp.zeros((), block_values.dtype))


def shards(a_values, a_rows, a_ks, a_count, t_panel):
    slot_count = a_values.shape[2]
    block_size = a_values.shape[3]
    inner_depth = t_panel.shape[0] // block_size
    panel_width = t_panel.shape[1]
    groups = lax.axis_size("row")
    values = a_values.reshape(1, slot_count, block_size, block_size)
    rows_here = a_rows.reshape(1, slot_count)
    inner_here = a_ks.reshape(1, slot_count)
    counts = a_count.reshape(1)
    zero_rows = jnp.zeros((groups * RB * block_size, panel_width), jnp.float32)
    partial_value = zero_rows
    offset = jnp.int32(0)
    piece_values = lax.all_gather(values, "row", axis=0, tiled=True)
    piece_rows = lax.all_gather(rows_here, "row", axis=0, tiled=True)
    piece_inner = lax.all_gather(inner_here, "row", axis=0, tiled=True)
    piece_counts = lax.all_gather(counts, "row", axis=0, tiled=True)
    piece_values = live_values(piece_values, piece_counts)
    for source in range(piece_values.shape[0]):
        dense_grid = jnp.zeros((RB, block_size, inner_depth, block_size), piece_values.dtype)
        dense_grid = dense_grid.at[piece_rows[source], :, piece_inner[source], :].add(
            piece_values[source]
        )
        result = jnp.dot(
            dense_grid.reshape(RB * block_size, inner_depth * block_size),
            t_panel,
            preferred_element_type=jnp.float32,
        )
        first_row = (offset + source) * (RB * block_size)
        partial_value = lax.dynamic_update_slice(
            partial_value, result, (first_row, jnp.zeros((), first_row.dtype))
        )
    summed = lax.psum_scatter(partial_value, ("layer", "col"), scatter_dimension=0, tiled=True)
    return (0.5 * summed).astype(jnp.bfloat16)


def solution(mesh):
    placed = (
        P("row", ("layer", "col"), None, None, None),
        P("row", ("layer", "col"), None),
        P("row", ("layer", "col"), None),
        P(("layer", "col"), "row"),
        P(("layer", "col"), "row"),
    )
    return jax.shard_map(
        shards, mesh=mesh, in_specs=placed, out_specs=P(("layer", "col"), "row"), check_vma=False
    )
```

profile of v0, /device:TPU:1, one launch (start us, length us, event | category | flops | bytes accessed | tf_op | source)
XLA Modules:
  0.0 341.8 jit_solution(10060311450433262915)
XLA Ops:
  6.5 0.7 all-gather.6.cloned.1.call-update
  7.3 0.0 reduce-scatter.2.cloned.1.call-start
  8.0 1.3 dynamic-slice
  9.2 0.7 bitcast_dynamic-update-slice_fusion
  9.9 14.1 %all-reduce.1 = s32[8]{0:T(128)S(1)} all-reduce(s32[8]{0:T(128)S(1)} %bitcast_dynamic-update-slice_fusion), channel_id=4, replica_groups=mesh['layer'=4,'row'=8,'col'=8] {'row'}, use_global_device_ids=true, to_apply=%add.1 | all-reduce | flops 8 | bytes 64
  24.0 12.2 %all-gather = s32[8,1,24]{2,1,0:T(1,128)S(1)} all-gather(s32[1,1,24]{2,1,0:T(1,128)} %param.6), channel_id=2, replica_groups=mesh['layer'=4,'row'=8,'col'=8] {'row'}, dimensions={0}, use_global_device_ids=true | all-gather | bytes 864 | tf_op jit(solution)/shard_map/all_gather | solution.py:28
  36.2 12.2 %all-gather.1 = s32[8,1,24]{2,1,0:T(1,128)S(1)} all-gather(s32[1,1,24]{2,1,0:T(1,128)} %param.7), channel_id=3, replica_groups=mesh['layer'=4,'row'=8,'col'=8] {'row'}, dimensions={0}, use_global_device_ids=true | all-gather | bytes 864 | tf_op jit(solution)/shard_map/all_gather | solution.py:29
  48.3 0.1 iota_compare_fusion
  48.4 39.1 %all-gather.6.cloned.1.call-done = bf16[8,1,24,128,128]{4,3,2,1,0:T(8,128)(2,1)} async-done(((bf16[1,1,24,128,128]{4,3,2,1,0:T(8,128)(2,1)}), bf16[8,1,24,128,128]{4,3,2,1,0:T(8,128)(2,1)}) %all-gather.6.cloned.1.call-update) | async-done | bytes 6291472 | tf_op jit(solution)/shard_map/all_gather | solution.py:27
  87.6 3.3 bitcast_select_fusion
  90.8 2.4 slice_bitcast_fusion
  93.3 3.0 broadcast.250.clone
  96.3 7.2 %scatter_fusion = bf16[4,128,32,128]{3,1,2,0:T(8,128)(2,1)} fusion(bf16[4,128,32,128]{3,1,2,0:T(8,128)(2,1)} %broadcast.250.clone, s32[24]{0:T(128)S(1)} %get-tuple-element.20, bf16[24,128,128]{2,1,0:T(8,128)(2,1)} %get-tuple-element.12), kind=kCustom, calls=%fused_computation | custom fusion | flops 393216 | bytes 2359488 | tf_op jit(solution)/shard_map/scatter-add | solution.py:34
  103.5 6.8 %copy.14 = bf16[4,128,32,128]{3,2,1,0:T(8,128)(2,1)} copy(bf16[4,128,32,128]{3,1,2,0:T(8,128)(2,1)} %scatter_fusion) | data formatting | bytes 8388608 | tf_op jit(solution)/shard_map/scatter-add | solution.py:34
  110.3 3.0 broadcast.250.clone.1
  113.3 6.9 %scatter_fusion.1 = bf16[4,128,32,128]{3,1,2,0:T(8,128)(2,1)} fusion(bf16[4,128,32,128]{3,1,2,0:T(8,128)(2,1)} %broadcast.250.clone.1, s32[24]{0:T(128)S(1)} %get-tuple-element.19, bf16[24,128,128]{2,1,0:T(8,128)(2,1)} %get-tuple-element.11), kind=kCustom, calls=%fused_computation.1 | custom fusion | flops 393216 | bytes 2359488 | tf_op jit(solution)/shard_map/scatter-add | solution.py:34
  120.2 6.9 %copy.15 = bf16[4,128,32,128]{3,2,1,0:T(8,128)(2,1)} copy(bf16[4,128,32,128]{3,1,2,0:T(8,128)(2,1)} %scatter_fusion.1) | data formatting | bytes 8388608 | tf_op jit(solution)/shard_map/scatter-add | solution.py:34
  127.1 3.0 broadcast.250.clone.2
  130.1 7.1 %scatter_fusion.2 = bf16[4,128,32,128]{3,1,2,0:T(8,128)(2,1)} fusion(bf16[4,128,32,128]{3,1,2,0:T(8,128)(2,1)} %broadcast.250.clone.2, s32[24]{0:T(128)S(1)} %get-tuple-element.18, bf16[24,128,128]{2,1,0:T(8,128)(2,1)} %get-tuple-element.10), kind=kCustom, calls=%fused_computation.2 | custom fusion | flops 393216 | bytes 2359488 | tf_op jit(solution)/shard_map/scatter-add | solution.py:34
  137.2 6.9 %copy.16 = bf16[4,128,32,128]{3,2,1,0:T(8,128)(2,1)} copy(bf16[4,128,32,128]{3,1,2,0:T(8,128)(2,1)} %scatter_fusion.2) | data formatting | bytes 8388608 | tf_op jit(solution)/shard_map/scatter-add | solution.py:34
  144.1 3.0 broadcast.250.clone.3
  147.0 6.9 %scatter_fusion.3 = bf16[4,128,32,128]{3,1,2,0:T(8,128)(2,1)} fusion(bf16[4,128,32,128]{3,1,2,0:T(8,128)(2,1)} %broadcast.250.clone.3, s32[24]{0:T(128)S(1)} %get-tuple-element.17, bf16[24,128,128]{2,1,0:T(8,128)(2,1)} %get-tuple-element.9), kind=kCustom, calls=%fused_computation.3 | custom fusion | flops 393216 | bytes 2359488 | tf_op jit(solution)/shard_map/scatter-add | solution.py:34
  153.9 6.8 %copy.17 = bf16[4,128,32,128]{3,2,1,0:T(8,128)(2,1)} copy(bf16[4,128,32,128]{3,1,2,0:T(8,128)(2,1)} %scatter_fusion.3) | data formatting | bytes 8388608 | tf_op jit(solution)/shard_map/scatter-add | solution.py:34
  160.8 3.0 broadcast.250.clone.4
  163.8 7.4 %scatter_fusion.4 = bf16[4,128,32,128]{3,1,2,0:T(8,128)(2,1)} fusion(bf16[4,128,32,128]{3,1,2,0:T(8,128)(2,1)} %broadcast.250.clone.4, s32[24]{0:T(128)S(1)} %get-tuple-element.16, bf16[24,128,128]{2,1,0:T(8,128)(2,1)} %get-tuple-element.8), kind=kCustom, calls=%fused_computation.4 | custom fusion | flops 393216 | bytes 2359488 | tf_op jit(solution)/shard_map/scatter-add | solution.py:34
  171.2 6.8 %copy.18 = bf16[4,128,32,128]{3,2,1,0:T(8,128)(2,1)} copy(bf16[4,128,32,128]{3,1,2,0:T(8,128)(2,1)} %scatter_fusion.4) | data formatting | bytes 8388608 | tf_op jit(solution)/shard_map/scatter-add | solution.py:34
  178.0 3.0 broadcast.250.clone.5
  181.0 6.9 %scatter_fusion.5 = bf16[4,128,32,128]{3,1,2,0:T(8,128)(2,1)} fusion(bf16[4,128,32,128]{3,1,2,0:T(8,128)(2,1)} %broadcast.250.clone.5, s32[24]{0:T(128)S(1)} %get-tuple-element.15, bf16[24,128,128]{2,1,0:T(8,128)(2,1)} %get-tuple-element.7), kind=kCustom, calls=%fused_computation.5 | custom fusion | flops 393216 | bytes 2359488 | tf_op jit(solution)/shard_map/scatter-add | solution.py:34
  187.9 6.9 %copy.19 = bf16[4,128,32,128]{3,2,1,0:T(8,128)(2,1)} copy(bf16[4,128,32,128]{3,1,2,0:T(8,128)(2,1)} %scatter_fusion.5) | data formatting | bytes 8388608 | tf_op jit(solution)/shard_map/scatter-add | solution.py:34
  194.8 3.0 broadcast.250.clone.6
  197.8 6.9 %scatter_fusion.6 = bf16[4,128,32,128]{3,1,2,0:T(8,128)(2,1)} fusion(bf16[4,128,32,128]{3,1,2,0:T(8,128)(2,1)} %broadcast.250.clone.6, s32[24]{0:T(128)S(1)} %get-tuple-element.14, bf16[24,128,128]{2,1,0:T(8,128)(2,1)} %get-tuple-element.6), kind=kCustom, calls=%fused_computation.6 | custom fusion | flops 393216 | bytes 2359488 | tf_op jit(solution)/shard_map/scatter-add | solution.py:34
  204.7 6.9 %copy.20 = bf16[4,128,32,128]{3,2,1,0:T(8,128)(2,1)} copy(bf16[4,128,32,128]{3,1,2,0:T(8,128)(2,1)} %scatter_fusion.6) | data formatting | bytes 8388608 | tf_op jit(solution)/shard_map/scatter-add | solution.py:34
  211.6 3.0 broadcast.250.clone.7
  214.6 6.5 %scatter_fusion.7 = bf16[4,128,32,128]{3,1,2,0:T(8,128)(2,1)} fusion(bf16[4,128,32,128]{3,1,2,0:T(8,128)(2,1)} %broadcast.250.clone.7, s32[24]{0:T(128)S(1)} %get-tuple-element.13, bf16[24,128,128]{2,1,0:T(8,128)(2,1)S(1)} %get-tuple-element.5), kind=kCustom, calls=%fused_computation.7 | custom fusion | flops 393216 | bytes 2359488 | tf_op jit(solution)/shard_map/scatter-add | solution.py:34
  221.1 5.0 %copy.21 = bf16[4,128,32,128]{3,2,1,0:T(8,128)(2,1)S(1)} copy(bf16[4,128,32,128]{3,1,2,0:T(8,128)(2,1)} %scatter_fusion.7) | data formatting | bytes 8388608 | tf_op jit(solution)/shard_map/scatter-add | solution.py:34
  226.2 1.3 fusion.21
  227.5 2.4 dynamic_update_slice.24
  229.9 1.3 copy-done.2
  231.2 2.2 fusion.24
  233.4 2.2 fusion.27
  235.6 2.2 fusion.30
  237.9 2.2 fusion.33
  240.0 2.2 fusion.36
  242.3 2.1 fusion.39
  244.4 2.2 fusion.42
  246.6 0.0 reduce-scatter.2.cloned.1.call-update
  246.6 86.6 %reduce-scatter.2.cloned.1.call-done = f32[128,256]{1,0:T(8,128)} async-done(((f32[4096,256]{1,0:T(8,128)}), f32[128,256]{1,0:T(8,128)}) %reduce-scatter.2.cloned.1.call-update) | async-done | bytes 131088 | tf_op jit(solution)/shard_map/reduce_scatter | solution.py:46
  333.2 1.5 multiply_convert_fusion
  (18 shorter events, 0.1 us)
Async XLA Ops:
  6.5 219.6 %copy-start = (bf16[4096,256]{1,0:T(8,128)(2,1)S(1)}, bf16[4096,256]{1,0:T(8,128)(2,1)}, u32[]{:S(2)}) copy-start(bf16[4096,256]{1,0:T(8,128)(2,1)} %param.9) | copy-start | bytes 6291460
  6.5 81.0 %all-gather.6.cloned.1.call-start = ((), (), s32[]{:S(2)}) async-start(), calls=%async_computation.2 | async-start | bytes 7077888 | tf_op jit(solution)/shard_map/all_gather | solution.py:27
  7.3 325.9 %reduce-scatter.2.cloned.1.call-start = ((), (), s32[]{:S(2)}) async-start(), calls=%async_computation.1 | async-start | bytes 4325376 | tf_op jit(solution)/shard_map/reduce_scatter | solution.py:46
  221.1 5.1 %copy-start.1 = (bf16[4,128,32,128]{3,2,1,0:T(8,128)(2,1)S(1)}, bf16[4,128,32,128]{3,2,1,0:T(8,128)(2,1)}, u32[]{:S(2)}) copy-start(bf16[4,128,32,128]{3,2,1,0:T(8,128)(2,1)} %copy.14) | copy-start | bytes 12582916
  227.5 3.7 %copy-start.2 = (bf16[4,128,32,128]{3,2,1,0:T(8,128)(2,1)S(1)}, bf16[4,128,32,128]{3,2,1,0:T(8,128)(2,1)}, u32[]{:S(2)}) copy-start(bf16[4,128,32,128]{3,2,1,0:T(8,128)(2,1)} %copy.15) | copy-start | bytes 12582916
  231.2 2.2 copy-start.3
  233.4 2.2 copy-start.4
  235.6 2.2 copy-start.5
  237.9 2.2 copy-start.6
  240.0 2.2 copy-start.7
Sparse Core Ops, SparseCore 0:
  9.1 78.3 all-gather.5
  246.7 86.4 reduce-scatter.1
where the time goes:
time: 346 us; the launch traced here: 342 us
  waiting for transfers between devices  126 us (36%)
  local copies, waits for them, and re-layouts  85.1 us (25%)
  other arithmetic  60.8 us (18%)
  blocking collectives  38.4 us (11%)
  matrix products  16.6 us (5%)
  between operations  14.3 us (4%)
    reduce_scatter x1, waiting for transfers between devices, shards(): lax.psum_scatter(partial_value, ('layer', 'col'), scatter_dimension=0, ti...  86.6 us
    scatter-add x8, other arithmetic, shards(): dense_grid.at[piece_rows[source], :, piece_inner[source], :]  55.9 us
    scatter-add x8, local copies, waits for them, and re-layouts, shards(): dense_grid.at[piece_rows[source], :, piece_inner[source], :]  53 us
    all_gather x1, waiting for transfers between devices, shards(): piece_values = lax.all_gather(values, 'row', axis=0, tiled=True)  39.1 us
    another operation x8, local copies, waits for them, and re-layouts  24 us
    dot_general x8, matrix products, shards(): jnp.dot(dense_grid.reshape(RB * block_size, inner_depth * block_size), t_...  16.6 us
    unnamed x1, blocking collectives  14.1 us
    all_gather x1, blocking collectives, shards(): piece_rows = lax.all_gather(rows_here, 'row', axis=0, tiled=True)  12.2 us
  transfers between devices with their start and end apart: 2, of which 2 were waited for; matrix products, arithmetic and copies ran while one was open for 1% of the time, Pallas kernels for 0%

commit v1 on v0

v1 whole, which is shorter than its diff:
```python
import functools

import jax
import jax.numpy as jnp
from jax import lax
from jax.experimental import pallas as pl
from jax.experimental.pallas import tpu as pltpu
from jax.sharding import PartitionSpec as P

MESH = pl.DeviceIdType.MESH
RB = 4
CH = 4


def kernel(dims, a_ref, rows_ref, ks_ref, count_ref, t_ref, out_ref,
           t_v, rxa, cmp_v, ring, meta, meta_all, tab, tab_s, run,
           mine, to_core, from_core, total, from_chip,
           loc_sem, a_send, a_recv, m_send, m_recv, g_send, g_recv, c_send, c_recv, x_send, x_recv):
    nx, nz, ny, slots, blk, live = dims
    chips = nx * ny
    sub = blk // nz
    blocks = nz * RB
    lx, rz, co = lax.axis_index("layer"), lax.axis_index("row"), lax.axis_index("col")
    cy, core = lax.div(co, 2), lax.rem(co, 2)
    chip = lx * ny + cy

    def on_z(o):
        return (lx, lax.rem(rz + o + nz, nz), co)

    def on_plane(q):
        dx, dy = lax.div(q, ny), lax.rem(q, ny)
        return lax.rem(lx + dx, nx), lax.rem(cy + dy, ny)

    def plane_device(q):
        x, y = on_plane(q)
        return (x, rz, 2 * y + core)

    other_core = (lx, rz, 2 * cy + 1 - core)

    t_copy = pltpu.make_async_copy(t_ref, t_v, loc_sem.at[0])
    t_copy.start()
    own_piece = pltpu.make_async_copy(
        a_ref.at[:, pl.ds(pl.multiple_of(rz * sub, sub), sub), :], rxa.at[pl.ds(rz * slots, slots)], loc_sem.at[1])
    own_piece.start()

    barrier = pltpu.get_barrier_semaphore()

    def greet_z(o, c_):
        pl.semaphore_signal(barrier, inc=1, device_id=on_z(o), device_id_type=MESH)
        return c_

    def greet_plane(q, c_):
        pl.semaphore_signal(barrier, inc=1, device_id=plane_device(q), device_id_type=MESH)
        return c_

    lax.fori_loop(1, nz, greet_z, 0)
    pl.semaphore_signal(barrier, inc=1, device_id=other_core, device_id_type=MESH)
    lax.fori_loop(1, chips, greet_plane, 0)

    meta[...] = jnp.zeros_like(meta)
    meta[0:1, 0:slots] = rows_ref[0]
    meta[1:2, 0:slots] = ks_ref[0]
    meta[2:3, :] = jnp.broadcast_to(count_ref[...], (1, 128))

    pl.semaphore_wait(barrier, nz - 1 + 1 + chips - 1)

    def a_copy(o):
        to = lax.rem(rz + o, nz)
        return pltpu.make_async_remote_copy(
            src_ref=a_ref.at[:, pl.ds(pl.multiple_of(to * sub, sub), sub), :],
            dst_ref=rxa.at[pl.ds(rz * slots, slots)],
            send_sem=a_send.at[o], recv_sem=a_recv.at[o], device_id=on_z(o), device_id_type=MESH)

    def m_copy(o):
        return pltpu.make_async_remote_copy(
            src_ref=meta, dst_ref=meta_all.at[rz],
            send_sem=m_send.at[o], recv_sem=m_recv.at[o], device_id=on_z(o), device_id_type=MESH)

    def a_arrived(o):
        source = lax.rem(rz - o + nz, nz)
        return pltpu.make_async_remote_copy(
            src_ref=a_ref.at[:, pl.ds(0, sub), :], dst_ref=rxa.at[pl.ds(source * slots, slots)],
            send_sem=a_send.at[o], recv_sem=a_recv.at[o], device_id=on_z(o), device_id_type=MESH)

    def m_arrived(o):
        source = lax.rem(rz - o + nz, nz)
        return pltpu.make_async_remote_copy(
            src_ref=meta, dst_ref=meta_all.at[source],
            send_sem=m_send.at[o], recv_sem=m_recv.at[o], device_id=on_z(o), device_id_type=MESH)

    def start_meta(o, c_):
        m_copy(o).start()
        return c_

    def start_pieces(o, c_):
        a_copy(o).start()
        return c_

    lax.fori_loop(1, nz, start_meta, 0)
    lax.fori_loop(1, nz, start_pieces, 0)

    meta_all[pl.ds(rz, 1)] = meta[...][None]

    def wait_meta(o, c_):
        m_arrived(o).wait_recv()
        m_copy(o).wait_send()
        return c_

    lax.fori_loop(1, nz, wait_meta, 0)

    row_of, col_of, count_of = meta_all[:, 0, :], meta_all[:, 1, :], meta_all[:, 2, :]
    lane = lax.broadcasted_iota(jnp.int32, (nz, 128), 1)
    group = lax.broadcasted_iota(jnp.int32, (nz, 128), 0)
    alive = lane < count_of
    row_key = jnp.where(alive, row_of, RB)
    rank = jnp.zeros((nz, 128), jnp.int32)
    in_row = jnp.zeros((nz, 128), jnp.int32)
    for g in range(nz - 1):
        rank = rank + jnp.where(group > g, jnp.broadcast_to(count_of[g:g + 1, :], (nz, 128)), 0)
    for s in range(slots):
        key = jnp.broadcast_to(row_key[:, s:s + 1], (nz, 128))
        same_before = jnp.where((key == row_key) & (lane > s), 1, 0)
        in_row = in_row + same_before
        rank = rank + same_before + jnp.where(key < row_key, 1, 0)
    rank = jnp.where(alive, rank, 1000)
    slot_at = jnp.zeros((nz, 128), jnp.int32)
    col_at = jnp.zeros((nz, 128), jnp.int32)
    keep_at = jnp.zeros((nz, 128), jnp.int32)
    upto = jnp.zeros((nz, 128), jnp.int32)
    equal = jnp.zeros((nz, 128), jnp.int32)
    for s in range(slots):
        hit = jnp.broadcast_to(rank[:, s:s + 1], (nz, 128)) == lane
        slot_at = slot_at + jnp.where(hit, group * slots + s, 0)
        col_at = col_at + jnp.where(hit, jnp.broadcast_to(col_of[:, s:s + 1], (nz, 128)), 0)
        keep_at = keep_at + jnp.where(hit, jnp.broadcast_to(in_row[:, s:s + 1], (nz, 128)), 0)
        key = jnp.broadcast_to(row_key[:, s:s + 1], (nz, 128))
        full_key = jnp.where(key < RB, group * RB + key, 1000)
        upto = upto + jnp.where(full_key <= lane, 1, 0)
        equal = equal + jnp.where(full_key == lane, 1, 0)
    last_at = jnp.sum(upto, axis=0, keepdims=True) - 1
    tab[0:1, :] = jnp.sum(slot_at, axis=0, keepdims=True)
    tab[1:2, :] = jnp.sum(col_at, axis=0, keepdims=True)
    tab[2:3, :] = jnp.sum(keep_at, axis=0, keepdims=True)
    tab[3:4, :] = jnp.where(jnp.sum(equal, axis=0, keepdims=True) > 0, last_at, live)
    tab[4:8, :] = jnp.zeros((4, 128), jnp.int32)
    table = pltpu.make_async_copy(tab, tab_s, loc_sem.at[2])
    table.start()
    run[live] = jnp.zeros(run.shape[1:], jnp.float32)
    table.wait()
    t_copy.wait()
    own_piece.wait()

    def wait_pieces(o, c_):
        a_arrived(o).wait_recv()
        a_copy(o).wait_send()
        return c_

    lax.fori_loop(1, nz, wait_pieces, 0)

    def compact(m, c_):
        cmp_v[m] = rxa[tab_s[0, m]]
        return c_

    lax.fori_loop(0, live, compact, 0, unroll=8)

    cs = live // CH

    def ring_copy(d, hop, c):
        src = cmp_v if hop == 1 else ring.at[3 * d + hop - 2]
        dst = ring.at[6] if hop == 4 else ring.at[3 * d + hop - 1]
        return pltpu.make_async_remote_copy(
            src_ref=src.at[pl.ds(cs * c, cs)], dst_ref=dst.at[pl.ds(cs * c, cs)],
            send_sem=g_send.at[d, hop - 1, c], recv_sem=g_recv.at[d, hop - 1, c],
            device_id=on_z(1 - 2 * d), device_id_type=MESH)

    def last_hop_chunk(d, c):
        return (c < CH // 2) == (d == 0)

    for c in range(CH):
        for d in (0, 1):
            ring_copy(d, 1, c).start()

    def multiply(pieces, c, carry):
        def item(i, acc):
            b = c * cs + i
            lhs = pieces[0][b] if len(pieces) == 1 else jnp.concatenate([p[b] for p in pieces], axis=0)
            term = jnp.dot(lhs, t_v[tab_s[1, b]], preferred_element_type=jnp.float32)
            acc = jnp.where(tab_s[2, b] > 0, acc, 0.0) + term
            run[b, 0:acc.shape[0]] = acc
            return acc
        return lax.fori_loop(0, cs, item, carry, unroll=8)

    def rows_in(t):
        return sub if t in (0, 4) else 2 * sub

    def core_copy(t):
        n = rows_in(t)
        return pltpu.make_async_remote_copy(
            src_ref=to_core.at[t, :, pl.ds(0, n)], dst_ref=from_core.at[t, :, pl.ds(0, n)],
            send_sem=c_send.at[t], recv_sem=c_recv.at[t], device_id=other_core, device_id_type=MESH)

    def split_rows(t):
        n = rows_in(t)

        def one(r, c_):
            mine[t, r, 0:n] = run[tab_s[3, 2 * r + core], 0:n]
            to_core[t, r, 0:n] = run[tab_s[3, 2 * r + 1 - core], 0:n]
            return c_

        lax.fori_loop(0, blocks // 2, one, 0, unroll=4)
        core_copy(t).start()

    def chip_copy(t, q):
        n = rows_in(t)
        x, y = on_plane(q)
        return pltpu.make_async_remote_copy(
            src_ref=total.at[t, x * ny + y, pl.ds(0, n)], dst_ref=from_chip.at[t, q, pl.ds(0, n)],
            send_sem=x_send.at[t, q], recv_sem=x_recv.at[t, q], device_id=(x, rz, 2 * y + core), device_id_type=MESH)

    def send_rows(t):
        n = rows_in(t)
        core_copy(t).wait_recv()

        def one(r, c_):
            total[t, r, 0:n] = mine[t, r, 0:n] + from_core[t, r, 0:n]
            return c_

        lax.fori_loop(0, chips, one, 0, unroll=4)

        def send(q, c_):
            chip_copy(t, q).start()
            return c_

        lax.fori_loop(1, chips, send, 0)

    def finish(t):
        n = rows_in(t)

        def wait(q, c_):
            chip_copy(t, q).wait_recv()
            return c_

        lax.fori_loop(1, chips, wait, 0)

        def add(q, acc):
            return acc + from_chip[t, q, 0:n]

        acc = lax.fori_loop(1, chips, add, total[t, chip, 0:n], unroll=5)
        acc = (0.5 * acc).astype(out_ref.dtype)
        for k in range(n // sub):
            shift = 0 if t == 0 else (t if k else nz - t)
            piece = lax.rem(rz + shift, nz)
            out_ref[pl.ds(pl.multiple_of(piece * sub, sub), sub), :] = acc[k * sub:(k + 1) * sub]

    width = t_v.shape[2]
    acc = jnp.zeros((sub, width), jnp.float32)
    for c in range(CH):
        acc = multiply([cmp_v], c, acc)
    split_rows(0)
    for t in (1, 2, 3):
        acc = jnp.zeros((2 * sub, width), jnp.float32)
        for c in range(CH):
            for d in (0, 1):
                ring_copy(d, t, c).wait_recv()
                if t < 3 or last_hop_chunk(d, c):
                    ring_copy(d, t + 1, c).start()
            acc = multiply([ring.at[t - 1], ring.at[3 + t - 1]], c, acc)
            if c == 1:
                send_rows(t - 1)
        split_rows(t)
    acc = jnp.zeros((sub, width), jnp.float32)
    for c in range(CH):
        ring_copy(0 if last_hop_chunk(0, c) else 1, 4, c).wait_recv()
        acc = multiply([ring.at[6]], c, acc)
        if c == 1:
            send_rows(3)
    split_rows(4)
    for t in (0, 1, 2):
        finish(t)
    send_rows(4)
    finish(3)
    finish(4)

    for d in (0, 1):
        for hop in (1, 2, 3, 4):
            for c in range(CH):
                if hop < 4 or last_hop_chunk(d, c):
                    ring_copy(d, hop, c).wait_send()
    for t in range(5):
        core_copy(t).wait_send()

        def sent(q, c_):
            chip_copy(t, q).wait_send()
            return c_

        lax.fori_loop(1, chips, sent, 0)


def shards(nx, nz, ny, a_values, a_rows, a_ks, a_count, t_panel):
    slots, blk = a_values.shape[2], a_values.shape[3]
    depth, width = t_panel.shape
    inner = depth // blk
    chips = nx * ny
    sub = blk // nz
    live = 64
    dma = pltpu.SemaphoreType.DMA
    any_spec = pl.BlockSpec(memory_space=pl.ANY)
    vmem_spec = pl.BlockSpec(memory_space=pltpu.VMEM)
    f32, i32, bf16 = jnp.float32, jnp.int32, jnp.bfloat16
    return pl.pallas_call(
        functools.partial(kernel, (nx, nz, ny, slots, blk, live)),
        out_shape=jax.ShapeDtypeStruct((blk, width), bf16),
        in_specs=[any_spec, vmem_spec, vmem_spec, vmem_spec, any_spec],
        out_specs=vmem_spec,
        scratch_shapes=[
            pltpu.VMEM((inner, blk, width), bf16),
            pltpu.VMEM((nz * slots, sub, blk), bf16),
            pltpu.VMEM((live, sub, blk), bf16),
            pltpu.VMEM((7, live, sub, blk), bf16),
            pltpu.VMEM((8, 128), i32),
            pltpu.VMEM((nz, 8, 128), i32),
            pltpu.VMEM((8, 128), i32),
            pltpu.SMEM((8, 128), i32),
            pltpu.VMEM((live + 1, 2 * sub, width), f32),
            pltpu.VMEM((5, chips, 2 * sub, width), f32),
            pltpu.VMEM((5, chips, 2 * sub, width), f32),
            pltpu.VMEM((5, chips, 2 * sub, width), f32),
            pltpu.VMEM((5, chips, 2 * sub, width), f32),
            pltpu.VMEM((5, chips, 2 * sub, width), f32),
            dma((3,)), dma((nz,)), dma((nz,)), dma((nz,)), dma((nz,)),
            dma((2, 4, CH)), dma((2, 4, CH)), dma((5,)), dma((5,)), dma((5, chips)), dma((5, chips)),
        ],
        compiler_params=pltpu.CompilerParams(
            collective_id=0, has_side_effects=True, vmem_limit_bytes=40 * 2**20),
        cost_estimate=pl.CostEstimate(flops=2 * live * blk * blk * width, bytes_accessed=4 * 2**20, transcendentals=0),
    )(a_values.reshape(slots, blk, blk), a_rows.reshape(1, 1, slots), a_ks.reshape(1, 1, slots), a_count,
      t_panel.reshape(inner, blk, width))


def solution(mesh):
    placed = (
        P("row", ("layer", "col"), None, None, None),
        P("row", ("layer", "col"), None),
        P("row", ("layer", "col"), None),
        P(("layer", "col"), "row"),
        P(("layer", "col"), "row"),
    )
    nx, nz, ny = mesh.shape["layer"], mesh.shape["row"], mesh.shape["col"] // 2
    return jax.shard_map(
        functools.partial(shards, nx, nz, ny),
        mesh=mesh, in_specs=placed, out_specs=P(("layer", "col"), "row"), check_vma=False
    )
```

time: 346 us -> 73.1 us (0.21); the launches traced: 342 us -> 72.9 us
  waiting for transfers between devices: 126 us -> 0 us
  local copies, waits for them, and re-layouts: 85.1 us -> 4.66 us
  Pallas kernels: 0 us -> 67.6 us
  other arithmetic: 60.8 us -> 0 us
  blocking collectives: 38.4 us -> 0 us
  matrix products: 16.6 us -> 0 us
  between operations: 14.3 us -> 0.67 us
    reduce_scatter x1 -> x0, waiting for transfers between devices: 86.6 us -> none  [shards(): lax.psum_scatter(partial_value, ('layer', 'col'), scatter_dimension=0, ti...]
    pallas_call x0 -> x1, Pallas kernels: none -> 67.6 us  [shards(): pl.pallas_call(functools.partial(kernel, (nx, nz, ny, slots, blk, live)),...]
    scatter-add x8 -> x0, other arithmetic: 55.9 us -> none  [shards(): dense_grid.at[piece_rows[source], :, piece_inner[source], :]]
    scatter-add x8 -> x0, local copies, waits for them, and re-layouts: 53 us -> none  [shards(): dense_grid.at[piece_rows[source], :, piece_inner[source], :]]
    all_gather x1 -> x0, waiting for transfers between devices: 39.1 us -> none  [shards(): piece_values = lax.all_gather(values, 'row', axis=0, tiled=True)]
    all_gather x2 -> x0, blocking collectives: 24.4 us -> none  [the longest x1 12.2 us: shards(): piece_rows = lax.all_gather(rows_here, 'row', axis=0, tiled=True)]
    another operation x8 -> x0, local copies, waits for them, and re-layouts: 24 us -> none
    dot_general x8 -> x0, matrix products: 16.6 us -> none  [shards(): jnp.dot(dense_grid.reshape(RB * block_size, inner_depth * block_size), t_...]
  transfers between devices with their start and end apart: 2 -> 0, of which waited for: 2 -> 0; matrix products, arithmetic and copies ran while one was open for 1% -> 0% of each run, Pallas kernels for 0% -> 0%
where the time goes in v1:
time: 73.1 us; the launch traced here: 72.9 us
  Pallas kernels  67.6 us (92%)
  local copies, waits for them, and re-layouts  4.66 us (6%)
    pallas_call x1, Pallas kernels, shards(): pl.pallas_call(functools.partial(kernel, (nx, nz, ny, slots, blk, live)),...  67.6 us
    unnamed x9, local copies, waits for them, and re-layouts  4.66 us

profile of v1, /device:TPU:1, one launch (start us, length us, event | category | flops | bytes accessed | tf_op | source)
XLA Modules:
  0.0 72.9 jit_solution(16576921972397579811)
XLA Ops:
  0.7 0.0 copy-start
  0.7 1.6 %copy-done = bf16[4096,256]{1,0:T(8,128)(2,1)S(1)} copy-done((bf16[4096,256]{1,0:T(8,128)(2,1)S(1)}, bf16[4096,256]{1,0:T(8,128)(2,1)}, u32[]{:S(2)}) %copy-start) | copy-done | bytes 2097176
  2.2 0.0 copy-start.1
  2.2 1.1 %copy-done.1 = bf16[1,1,24,128,128]{4,3,2,1,0:T(8,128)(2,1)S(1)} copy-done((bf16[1,1,24,128,128]{4,3,2,1,0:T(8,128)(2,1)S(1)}, bf16[1,1,24,128,128]{4,3,2,1,0:T(8,128)(2,1)}, u32[]{:S(2)}) %copy-start.1) | copy-done | bytes 786456
  3.4 0.0 copy-start.2
  3.4 0.7 copy-done.2
  4.0 0.0 copy-start.3
  4.0 0.7 copy-done.3
  4.7 67.6 %shard_map.55 = bf16[128,256]{1,0:T(8,128)(2,1)S(1)} custom-call(bf16[24,128,128]{2,1,0:T(8,128)(2,1)S(1)} %bitcast.3, s32[1,1,24]{2,1,0:T(1,128)S(1)} %copy-done.2, s32[1,1,24]{2,1,0:T(1,128)S(1)} %copy-done.3, s32[1,1]{1,0:T(1,128)S(6)} %copy.7.count_ref, bf16[32,128,256]{2,1,0:T(8,128)(2,1)S(1)} %bitcast.2), custom_call_target="tpu_custom_call" | custom-call | flops 536870912 | bytes 4194304 | tf_op jit(solution)/shard_map/pallas_call | solution.py:310
  72.3 0.6 copy.8
Async XLA Ops:
  0.7 1.6 %copy-start = (bf16[4096,256]{1,0:T(8,128)(2,1)S(1)}, bf16[4096,256]{1,0:T(8,128)(2,1)}, u32[]{:S(2)}) copy-start(bf16[4096,256]{1,0:T(8,128)(2,1)} %param.9) | copy-start | bytes 6291460
  2.2 1.1 %copy-start.1 = (bf16[1,1,24,128,128]{4,3,2,1,0:T(8,128)(2,1)S(1)}, bf16[1,1,24,128,128]{4,3,2,1,0:T(8,128)(2,1)}, u32[]{:S(2)}) copy-start(bf16[1,1,24,128,128]{4,3,2,1,0:T(8,128)(2,1)} %param.5) | copy-start | bytes 2359300
  3.4 0.7 copy-start.2
  4.0 0.7 copy-start.3

commit v2 on v1

--- a/solution.py
+++ b/solution.py
@@ -14,7 +14,7 @@
 
 def kernel(dims, a_ref, rows_ref, ks_ref, count_ref, t_ref, out_ref,
            t_v, rxa, cmp_v, ring, meta, meta_all, tab, tab_s, run,
-           mine, to_core, from_core, total, from_chip,
+           mine, to_core, from_core, coded, from_chip, rows_v, ks_v, count_v,
            loc_sem, a_send, a_recv, m_send, m_recv, g_send, g_recv, c_send, c_recv, x_send, x_recv):
     nx, nz, ny, slots, blk, live = dims
     chips = nx * ny
@@ -37,12 +37,6 @@
 
     other_core = (lx, rz, 2 * cy + 1 - core)
 
-    t_copy = pltpu.make_async_copy(t_ref, t_v, loc_sem.at[0])
-    t_copy.start()
-    own_piece = pltpu.make_async_copy(
-        a_ref.at[:, pl.ds(pl.multiple_of(rz * sub, sub), sub), :], rxa.at[pl.ds(rz * slots, slots)], loc_sem.at[1])
-    own_piece.start()
-
     barrier = pltpu.get_barrier_semaphore()
 
     def greet_z(o, c_):
@@ -57,10 +51,16 @@
     pl.semaphore_signal(barrier, inc=1, device_id=other_core, device_id_type=MESH)
     lax.fori_loop(1, chips, greet_plane, 0)
 
+    about = [pltpu.make_async_copy(src, dst, loc_sem.at[3 + k])
+             for k, (src, dst) in enumerate(((rows_ref, rows_v), (ks_ref, ks_v), (count_ref, count_v)))]
+    for copy in about:
+        copy.start()
     meta[...] = jnp.zeros_like(meta)
-    meta[0:1, 0:slots] = rows_ref[0]
-    meta[1:2, 0:slots] = ks_ref[0]
-    meta[2:3, :] = jnp.broadcast_to(count_ref[...], (1, 128))
+    for copy in about:
+        copy.wait()
+    meta[0:1, 0:slots] = rows_v[0]
+    meta[1:2, 0:slots] = ks_v[0]
+    meta[2:3, :] = jnp.broadcast_to(count_v[...], (1, 128))
 
     pl.semaphore_wait(barrier, nz - 1 + 1 + chips - 1)
 
@@ -69,24 +69,12 @@
         return pltpu.make_async_remote_copy(
             src_ref=a_ref.at[:, pl.ds(pl.multiple_of(to * sub, sub), sub), :],
             dst_ref=rxa.at[pl.ds(rz * slots, slots)],
-            send_sem=a_send.at[o], recv_sem=a_recv.at[o], device_id=on_z(o), device_id_type=MESH)
+            send_sem=a_send.at[0], recv_sem=a_recv.at[0], device_id=on_z(o), device_id_type=MESH)
 
     def m_copy(o):
         return pltpu.make_async_remote_copy(
             src_ref=meta, dst_ref=meta_all.at[rz],
-            send_sem=m_send.at[o], recv_sem=m_recv.at[o], device_id=on_z(o), device_id_type=MESH)
-
-    def a_arrived(o):
-        source = lax.rem(rz - o + nz, nz)
-        return pltpu.make_async_remote_copy(
-            src_ref=a_ref.at[:, pl.ds(0, sub), :], dst_ref=rxa.at[pl.ds(source * slots, slots)],
-            send_sem=a_send.at[o], recv_sem=a_recv.at[o], device_id=on_z(o), device_id_type=MESH)
-
-    def m_arrived(o):
-        source = lax.rem(rz - o + nz, nz)
-        return pltpu.make_async_remote_copy(
-            src_ref=meta, dst_ref=meta_all.at[source],
-            send_sem=m_send.at[o], recv_sem=m_recv.at[o], device_id=on_z(o), device_id_type=MESH)
+            send_sem=m_send.at[0], recv_sem=m_recv.at[0], device_id=on_z(o), device_id_type=MESH)
 
     def start_meta(o, c_):
         m_copy(o).start()
@@ -98,15 +86,19 @@
 
     lax.fori_loop(1, nz, start_meta, 0)
     lax.fori_loop(1, nz, start_pieces, 0)
+    t_copy = pltpu.make_async_copy(t_ref, t_v, loc_sem.at[0])
+    own_piece = pltpu.make_async_copy(
+        a_ref.at[:, pl.ds(pl.multiple_of(rz * sub, sub), sub), :], rxa.at[pl.ds(rz * slots, slots)], loc_sem.at[1])
+
+    own_piece.start()
+    t_copy.start()
 
     meta_all[pl.ds(rz, 1)] = meta[...][None]
 
-    def wait_meta(o, c_):
-        m_arrived(o).wait_recv()
-        m_copy(o).wait_send()
-        return c_
-
-    lax.fori_loop(1, nz, wait_meta, 0)
+    m_all = pltpu.make_async_remote_copy(
+        src_ref=meta_all.at[pl.ds(0, nz - 1)], dst_ref=meta_all.at[pl.ds(0, nz - 1)],
+        send_sem=m_send.at[0], recv_sem=m_recv.at[0], device_id=other_core, device_id_type=MESH)
+    m_all.wait_recv()
 
     row_of, col_of, count_of = meta_all[:, 0, :], meta_all[:, 1, :], meta_all[:, 2, :]
     lane = lax.broadcasted_iota(jnp.int32, (nz, 128), 1)
@@ -150,18 +142,15 @@
     t_copy.wait()
     own_piece.wait()
 
-    def wait_pieces(o, c_):
-        a_arrived(o).wait_recv()
-        a_copy(o).wait_send()
-        return c_
-
-    lax.fori_loop(1, nz, wait_pieces, 0)
+    a_all = pltpu.make_async_remote_copy(
+        src_ref=rxa.at[pl.ds(0, (nz - 1) * slots)], dst_ref=rxa.at[pl.ds(0, (nz - 1) * slots)],
+        send_sem=a_send.at[0], recv_sem=a_recv.at[0], device_id=other_core, device_id_type=MESH)
+    a_all.wait_recv()
 
     def compact(m, c_):
         cmp_v[m] = rxa[tab_s[0, m]]
         return c_
 
-    lax.fori_loop(0, live, compact, 0, unroll=8)
 
     cs = live // CH
 
@@ -170,13 +159,14 @@
         dst = ring.at[6] if hop == 4 else ring.at[3 * d + hop - 1]
         return pltpu.make_async_remote_copy(
             src_ref=src.at[pl.ds(cs * c, cs)], dst_ref=dst.at[pl.ds(cs * c, cs)],
-            send_sem=g_send.at[d, hop - 1, c], recv_sem=g_recv.at[d, hop - 1, c],
+            send_sem=g_send.at[0], recv_sem=g_recv.at[d, hop - 1, c],
             device_id=on_z(1 - 2 * d), device_id_type=MESH)
 
     def last_hop_chunk(d, c):
         return (c < CH // 2) == (d == 0)
 
     for c in range(CH):
+        lax.fori_loop(cs * c, cs * (c + 1), compact, 0, unroll=8)
         for d in (0, 1):
             ring_copy(d, 1, c).start()
 
@@ -197,7 +187,7 @@
         n = rows_in(t)
         return pltpu.make_async_remote_copy(
             src_ref=to_core.at[t, :, pl.ds(0, n)], dst_ref=from_core.at[t, :, pl.ds(0, n)],
-            send_sem=c_send.at[t], recv_sem=c_recv.at[t], device_id=other_core, device_id_type=MESH)
+            send_sem=c_send.at[0], recv_sem=c_recv.at[t], device_id=other_core, device_id_type=MESH)
 
     def split_rows(t):
         n = rows_in(t)
@@ -211,18 +201,33 @@
         core_copy(t).start()
 
     def chip_copy(t, q):
-        n = rows_in(t)
+        n = 2 * rows_in(t) + sub
         x, y = on_plane(q)
         return pltpu.make_async_remote_copy(
-            src_ref=total.at[t, x * ny + y, pl.ds(0, n)], dst_ref=from_chip.at[t, q, pl.ds(0, n)],
-            send_sem=x_send.at[t, q], recv_sem=x_recv.at[t, q], device_id=(x, rz, 2 * y + core), device_id_type=MESH)
+            src_ref=coded.at[t, x * ny + y, pl.ds(0, n)], dst_ref=from_chip.at[t, q, pl.ds(0, n)],
+            send_sem=x_send.at[t], recv_sem=x_recv.at[t], device_id=(x, rz, 2 * y + core), device_id_type=MESH)
+
+    def chips_all(t):
+        n = 2 * rows_in(t) + sub
+        return pltpu.make_async_remote_copy(
+            src_ref=coded.at[t, pl.ds(1, chips - 1), pl.ds(0, n)], dst_ref=from_chip.at[t, pl.ds(1, chips - 1), pl.ds(0, n)],
+            send_sem=x_send.at[t], recv_sem=x_recv.at[t], device_id=other_core, device_id_type=MESH)
 
     def send_rows(t):
         n = rows_in(t)
         core_copy(t).wait_recv()
 
         def one(r, c_):
-            total[t, r, 0:n] = mine[t, r, 0:n] + from_core[t, r, 0:n]
+            value = mine[t, r, 0:n] + from_core[t, r, 0:n]
+            left, right = value[:, 0:128], value[:, 128:256]
+            top = jnp.max(jnp.maximum(jnp.abs(left), jnp.abs(right)), axis=0, keepdims=True)
+            power = jnp.floor(jnp.log2(jnp.maximum(top, 1e-30)) + 1.001)
+            up = jnp.exp2(15.0 - power)
+            for k, half in enumerate((left, right)):
+                fixed = jnp.clip(jnp.round(half * up), -32767.0, 32767.0)
+                coded[t, r, k * n:(k + 1) * n] = fixed.astype(jnp.int32).astype(jnp.int16)
+            power = jnp.broadcast_to(power, (sub, 128))
+            coded[t, r, 2 * n:2 * n + sub] = power.astype(jnp.int32).astype(jnp.int16)
             return c_
 
         lax.fori_loop(0, chips, one, 0, unroll=4)
@@ -236,21 +241,21 @@
     def finish(t):
         n = rows_in(t)
 
-        def wait(q, c_):
-            chip_copy(t, q).wait_recv()
-            return c_
-
-        lax.fori_loop(1, chips, wait, 0)
+        chips_all(t).wait_recv()
 
         def add(q, acc):
-            return acc + from_chip[t, q, 0:n]
-
-        acc = lax.fori_loop(1, chips, add, total[t, chip, 0:n], unroll=5)
-        acc = (0.5 * acc).astype(out_ref.dtype)
+            fixed = from_chip[t, q, 0:2 * n + sub].astype(jnp.int32).astype(jnp.float32)
+            down = jnp.exp2(fixed[2 * n:2 * n + 1] - 15.0)
+            return acc[0] + fixed[0:n] * down, acc[1] + fixed[n:2 * n] * down
+
+        own = mine[t, chip, 0:n] + from_core[t, chip, 0:n]
+        acc = lax.fori_loop(1, chips, add, (own[:, 0:128], own[:, 128:256]), unroll=5)
+        acc = [(0.5 * half).astype(out_ref.dtype) for half in acc]
         for k in range(n // sub):
             shift = 0 if t == 0 else (t if k else nz - t)
             piece = lax.rem(rz + shift, nz)
-            out_ref[pl.ds(pl.multiple_of(piece * sub, sub), sub), :] = acc[k * sub:(k + 1) * sub]
+            for h, half in enumerate(acc):
+                out_ref[pl.ds(pl.multiple_of(piece * sub, sub), sub), h * 128:(h + 1) * 128] = half[k * sub:(k + 1) * sub]
 
     width = t_v.shape[2]
     acc = jnp.zeros((sub, width), jnp.float32)
@@ -281,19 +286,16 @@
     finish(3)
     finish(4)
 
-    for d in (0, 1):
-        for hop in (1, 2, 3, 4):
-            for c in range(CH):
-                if hop < 4 or last_hop_chunk(d, c):
-                    ring_copy(d, hop, c).wait_send()
+    m_all.wait_send()
+    a_all.wait_send()
+    pltpu.make_async_remote_copy(
+        src_ref=ring, dst_ref=ring, send_sem=g_send.at[0], recv_sem=g_recv.at[0, 0, 0],
+        device_id=other_core, device_id_type=MESH).wait_send()
+    pltpu.make_async_remote_copy(
+        src_ref=to_core.at[pl.ds(0, 4)], dst_ref=to_core.at[pl.ds(0, 4)], send_sem=c_send.at[0], recv_sem=c_recv.at[0],
+        device_id=other_core, device_id_type=MESH).wait_send()
     for t in range(5):
-        core_copy(t).wait_send()
-
-        def sent(q, c_):
-            chip_copy(t, q).wait_send()
-            return c_
-
-        lax.fori_loop(1, chips, sent, 0)
+        chips_all(t).wait_send()
 
 
 def shards(nx, nz, ny, a_values, a_rows, a_ks, a_count, t_panel):
@@ -310,7 +312,7 @@
     return pl.pallas_call(
         functools.partial(kernel, (nx, nz, ny, slots, blk, live)),
         out_shape=jax.ShapeDtypeStruct((blk, width), bf16),
-        in_specs=[any_spec, vmem_spec, vmem_spec, vmem_spec, any_spec],
+        in_specs=[any_spec] * 5,
         out_specs=vmem_spec,
         scratch_shapes=[
             pltpu.VMEM((inner, blk, width), bf16),
@@ -325,13 +327,14 @@
             pltpu.VMEM((5, chips, 2 * sub, width), f32),
             pltpu.VMEM((5, chips, 2 * sub, width), f32),
             pltpu.VMEM((5, chips, 2 * sub, width), f32),
-            pltpu.VMEM((5, chips, 2 * sub, width), f32),
-            pltpu.VMEM((5, chips, 2 * sub, width), f32),
-            dma((3,)), dma((nz,)), dma((nz,)), dma((nz,)), dma((nz,)),
-            dma((2, 4, CH)), dma((2, 4, CH)), dma((5,)), dma((5,)), dma((5, chips)), dma((5, chips)),
+            pltpu.VMEM((5, chips, 5 * sub, 128), jnp.int16),
+            pltpu.VMEM((5, chips, 5 * sub, 128), jnp.int16),
+            pltpu.VMEM((1, 1, slots), i32), pltpu.VMEM((1, 1, slots), i32), pltpu.VMEM((1, 1), i32),
+            dma((6,)), dma((1,)), dma((1,)), dma((1,)), dma((1,)),
+            dma((1,)), dma((2, 4, CH)), dma((1,)), dma((5,)), dma((5,)), dma((5,)),
         ],
         compiler_params=pltpu.CompilerParams(
-            collective_id=0, has_side_effects=True, vmem_limit_bytes=40 * 2**20),
+            collective_id=0, has_side_effects=True, vmem_limit_bytes=60 * 2**20),
         cost_estimate=pl.CostEstimate(flops=2 * live * blk * blk * width, bytes_accessed=4 * 2**20, transcendentals=0),
     )(a_values.reshape(slots, blk, blk), a_rows.reshape(1, 1, slots), a_ks.reshape(1, 1, slots), a_count,
       t_panel.reshape(inner, blk, width))

time: 73.1 us -> 65.5 us (0.90)
  Pallas kernels: 67.6 us -> 63.2 us
  local copies, waits for them, and re-layouts: 4.66 us -> 1.47 us
    pallas_call x1, Pallas kernels: 67.6 us -> 63.2 us  [shards(): pl.pallas_call(functools.partial(kernel, (nx, nz, ny, slots, blk, live)),...]
    unnamed x9 -> x1, local copies, waits for them, and re-layouts: 4.66 us -> 1.47 us
where the time goes in v2:
time: 65.5 us; the launch traced here: 65.4 us
  Pallas kernels  63.2 us (96%)
  local copies, waits for them, and re-layouts  1.47 us (2%)
  between operations  0.66 us (1%)
    pallas_call x1, Pallas kernels, shards(): pl.pallas_call(functools.partial(kernel, (nx, nz, ny, slots, blk, live)),...  63.2 us
    unnamed x1, local copies, waits for them, and re-layouts  1.47 us

profile of v2, /device:TPU:1, one launch (start us, length us, event | category | flops | bytes accessed | tf_op | source)
XLA Modules:
  0.0 65.4 jit_solution(7797218276737123879)
XLA Ops:
  0.7 63.2 %shard_map.55 = bf16[128,256]{1,0:T(8,128)(2,1)} custom-call(bf16[24,128,128]{2,1,0:T(8,128)(2,1)} %bitcast.3, s32[1,1,24]{2,1,0:T(1,128)} %rows_ref.1, s32[1,1,24]{2,1,0:T(1,128)} %ks_ref.1, s32[1,1]{1,0:T(1,128)S(6)} %copy.7.count_ref, bf16[32,128,256]{2,1,0:T(8,128)(2,1)} %bitcast.2), custom_call_target="tpu_custom_call" | custom-call | flops 536870912 | bytes 4194304 | tf_op jit(solution)/shard_map/pallas_call | solution.py:312
  63.9 1.5 %copy.8 = bf16[128,256]{1,0:T(8,128)(2,1)} copy(bf16[128,256]{1,0:T(8,128)(2,1)} %shard_map.55) | data formatting | bytes 131072

commit v3 on v2

--- a/solution.py
+++ b/solution.py
@@ -12,9 +12,9 @@
 CH = 4
 
 
-def kernel(dims, a_ref, rows_ref, ks_ref, count_ref, t_ref, out_ref,
-           t_v, rxa, cmp_v, ring, meta, meta_all, tab, tab_s, run,
-           mine, to_core, from_core, coded, from_chip, rows_v, ks_v, count_v,
+def kernel(dims, a_ref, meta, t_ref, out_ref,
+           t_v, rxa, cmp_v, ring, meta_all, tab, tab_s, run,
+           mine, to_core, from_core, coded, from_chip,
            loc_sem, a_send, a_recv, m_send, m_recv, g_send, g_recv, c_send, c_recv, x_send, x_recv):
     nx, nz, ny, slots, blk, live = dims
     chips = nx * ny
@@ -28,7 +28,7 @@
         return (lx, lax.rem(rz + o + nz, nz), co)
 
     def on_plane(q):
-        dx, dy = lax.div(q, ny), lax.rem(q, ny)
+        dx, dy = q // ny, q % ny
         return lax.rem(lx + dx, nx), lax.rem(cy + dy, ny)
 
     def plane_device(q):
@@ -37,30 +37,18 @@
 
     other_core = (lx, rz, 2 * cy + 1 - core)
 
+    far_first = sorted(range(1, chips), key=lambda q: -min(q // ny, nx - q // ny) - min(q % ny, ny - q % ny))
+
     barrier = pltpu.get_barrier_semaphore()
 
     def greet_z(o, c_):
         pl.semaphore_signal(barrier, inc=1, device_id=on_z(o), device_id_type=MESH)
         return c_
 
-    def greet_plane(q, c_):
-        pl.semaphore_signal(barrier, inc=1, device_id=plane_device(q), device_id_type=MESH)
-        return c_
-
     lax.fori_loop(1, nz, greet_z, 0)
     pl.semaphore_signal(barrier, inc=1, device_id=other_core, device_id_type=MESH)
-    lax.fori_loop(1, chips, greet_plane, 0)
-
-    about = [pltpu.make_async_copy(src, dst, loc_sem.at[3 + k])
-             for k, (src, dst) in enumerate(((rows_ref, rows_v), (ks_ref, ks_v), (count_ref, count_v)))]
-    for copy in about:
-        copy.start()
-    meta[...] = jnp.zeros_like(meta)
-    for copy in about:
-        copy.wait()
-    meta[0:1, 0:slots] = rows_v[0]
-    meta[1:2, 0:slots] = ks_v[0]
-    meta[2:3, :] = jnp.broadcast_to(count_v[...], (1, 128))
+    for q in far_first:
+        pl.semaphore_signal(barrier, inc=1, device_id=plane_device(q), device_id_type=MESH)
 
     pl.semaphore_wait(barrier, nz - 1 + 1 + chips - 1)
 
@@ -100,7 +88,8 @@
         send_sem=m_send.at[0], recv_sem=m_recv.at[0], device_id=other_core, device_id_type=MESH)
     m_all.wait_recv()
 
-    row_of, col_of, count_of = meta_all[:, 0, :], meta_all[:, 1, :], meta_all[:, 2, :]
+    row_of, col_of = meta_all[:, 0, :], meta_all[:, 1, :]
+    count_of = jnp.broadcast_to(meta_all[:, 2, 0:1], (nz, 128))
     lane = lax.broadcasted_iota(jnp.int32, (nz, 128), 1)
     group = lax.broadcasted_iota(jnp.int32, (nz, 128), 0)
     alive = lane < count_of
@@ -178,7 +167,7 @@
             acc = jnp.where(tab_s[2, b] > 0, acc, 0.0) + term
             run[b, 0:acc.shape[0]] = acc
             return acc
-        return lax.fori_loop(0, cs, item, carry, unroll=8)
+        return lax.fori_loop(0, cs, item, carry, unroll=cs)
 
     def rows_in(t):
         return sub if t in (0, 4) else 2 * sub
@@ -213,11 +202,12 @@
             src_ref=coded.at[t, pl.ds(1, chips - 1), pl.ds(0, n)], dst_ref=from_chip.at[t, pl.ds(1, chips - 1), pl.ds(0, n)],
             send_sem=x_send.at[t], recv_sem=x_recv.at[t], device_id=other_core, device_id_type=MESH)
 
-    def send_rows(t):
+    def send_rows(t, start, stop):
         n = rows_in(t)
-        core_copy(t).wait_recv()
-
-        def one(r, c_):
+
+        for q in far_first[start:stop]:
+            x, y = on_plane(q)
+            r = x * ny + y
             value = mine[t, r, 0:n] + from_core[t, r, 0:n]
             left, right = value[:, 0:128], value[:, 128:256]
             top = jnp.max(jnp.maximum(jnp.abs(left), jnp.abs(right)), axis=0, keepdims=True)
@@ -228,15 +218,8 @@
                 coded[t, r, k * n:(k + 1) * n] = fixed.astype(jnp.int32).astype(jnp.int16)
             power = jnp.broadcast_to(power, (sub, 128))
             coded[t, r, 2 * n:2 * n + sub] = power.astype(jnp.int32).astype(jnp.int16)
-            return c_
-
-        lax.fori_loop(0, chips, one, 0, unroll=4)
-
-        def send(q, c_):
+        for q in far_first[start:stop]:
             chip_copy(t, q).start()
-            return c_
-
-        lax.fori_loop(1, chips, send, 0)
 
     def finish(t):
         n = rows_in(t)
@@ -270,19 +253,26 @@
                 if t < 3 or last_hop_chunk(d, c):
                     ring_copy(d, t + 1, c).start()
             acc = multiply([ring.at[t - 1], ring.at[3 + t - 1]], c, acc)
-            if c == 1:
-                send_rows(t - 1)
+            if c == 2:
+                core_copy(t - 1).wait_recv()
+                send_rows(t - 1, 0, chips // 2)
+            if c == 3:
+                send_rows(t - 1, chips // 2, chips)
         split_rows(t)
     acc = jnp.zeros((sub, width), jnp.float32)
     for c in range(CH):
         ring_copy(0 if last_hop_chunk(0, c) else 1, 4, c).wait_recv()
         acc = multiply([ring.at[6]], c, acc)
+        if c == 0:
+            core_copy(3).wait_recv()
+            send_rows(3, 0, chips // 2)
         if c == 1:
-            send_rows(3)
+            send_rows(3, chips // 2, chips)
     split_rows(4)
     for t in (0, 1, 2):
         finish(t)
-    send_rows(4)
+    core_copy(4).wait_recv()
+    send_rows(4, 0, chips)
     finish(3)
     finish(4)
 
@@ -305,6 +295,10 @@
     chips = nx * ny
     sub = blk // nz
     live = 64
+    wide = ((0, 0), (0, 128 - slots))
+    meta = jnp.concatenate([
+        jnp.pad(a_rows.reshape(1, slots), wide), jnp.pad(a_ks.reshape(1, slots), wide),
+        jnp.pad(a_count, ((0, 5), (0, 127)))], axis=0)
     dma = pltpu.SemaphoreType.DMA
     any_spec = pl.BlockSpec(memory_space=pl.ANY)
     vmem_spec = pl.BlockSpec(memory_space=pltpu.VMEM)
@@ -312,14 +306,13 @@
     return pl.pallas_call(
         functools.partial(kernel, (nx, nz, ny, slots, blk, live)),
         out_shape=jax.ShapeDtypeStruct((blk, width), bf16),
-        in_specs=[any_spec] * 5,
+        in_specs=[any_spec, vmem_spec, any_spec],
         out_specs=vmem_spec,
         scratch_shapes=[
             pltpu.VMEM((inner, blk, width), bf16),
             pltpu.VMEM((nz * slots, sub, blk), bf16),
             pltpu.VMEM((live, sub, blk), bf16),
             pltpu.VMEM((7, live, sub, blk), bf16),
-            pltpu.VMEM((8, 128), i32),
             pltpu.VMEM((nz, 8, 128), i32),
             pltpu.VMEM((8, 128), i32),
             pltpu.SMEM((8, 128), i32),
@@ -329,15 +322,13 @@
             pltpu.VMEM((5, chips, 2 * sub, width), f32),
             pltpu.VMEM((5, chips, 5 * sub, 128), jnp.int16),
             pltpu.VMEM((5, chips, 5 * sub, 128), jnp.int16),
-            pltpu.VMEM((1, 1, slots), i32), pltpu.VMEM((1, 1, slots), i32), pltpu.VMEM((1, 1), i32),
-            dma((6,)), dma((1,)), dma((1,)), dma((1,)), dma((1,)),
+            dma((3,)), dma((1,)), dma((1,)), dma((1,)), dma((1,)),
             dma((1,)), dma((2, 4, CH)), dma((1,)), dma((5,)), dma((5,)), dma((5,)),
         ],
         compiler_params=pltpu.CompilerParams(
-            collective_id=0, has_side_effects=True, vmem_limit_bytes=60 * 2**20),
+            collective_id=0, has_side_effects=True, vmem_limit_bytes=54784 * 2**10),
         cost_estimate=pl.CostEstimate(flops=2 * live * blk * blk * width, bytes_accessed=4 * 2**20, transcendentals=0),
-    )(a_values.reshape(slots, blk, blk), a_rows.reshape(1, 1, slots), a_ks.reshape(1, 1, slots), a_count,
-      t_panel.reshape(inner, blk, width))
+    )(a_values.reshape(slots, blk, blk), meta, t_panel.reshape(inner, blk, width))
 
 
 def solution(mesh):

time: 65.5 us -> 63.5 us (0.969)
  Pallas kernels: 63.2 us -> 61.5 us
  local copies, waits for them, and re-layouts: 1.47 us -> 0.63 us
  other arithmetic: 0 us -> 0.68 us
    pallas_call x1, Pallas kernels: 63.2 us -> 61.5 us  [shards(): pl.pallas_call(functools.partial(kernel, (nx, nz, ny, slots, blk, live)),...]
    unnamed x1, local copies, waits for them, and re-layouts: 1.47 us -> 0.63 us
    concatenate x0 -> x1, other arithmetic: none -> 0.68 us  [shards(): jnp.concatenate([jnp.pad(a_rows.reshape(1, slots), wide), jnp.pad(a_ks.re...]
where the time goes in v3:
time: 63.5 us; the launch traced here: 63.4 us
  Pallas kernels  61.5 us (97%)
  other arithmetic  0.68 us (1%)
  between operations  0.66 us (1%)
    pallas_call x1, Pallas kernels, shards(): pl.pallas_call(functools.partial(kernel, (nx, nz, ny, slots, blk, live)),...  61.5 us

profile of v3, /device:TPU:1, one launch (start us, length us, event | category | flops | bytes accessed | tf_op | source)
XLA Modules:
  0.0 63.4 jit_solution(15331999447315885612)
XLA Ops:
  0.7 0.7 %pad_add_fusion.meta = s32[8,128]{1,0:T(8,128)S(1)} fusion(s32[1,1]{1,0:T(1,128)S(6)} %copy.7, s32[1,24]{1,0:T(1,128)} %bitcast.6, s32[1,24]{1,0:T(1,128)} %bitcast.7), kind=kLoop, calls=%fused_computation | loop fusion | flops 2048 | bytes 4292 | tf_op jit(solution)/shard_map/concatenate | solution.py:299
  1.3 61.5 %shard_map.55 = bf16[128,256]{1,0:T(8,128)(2,1)S(1)} custom-call(bf16[24,128,128]{2,1,0:T(8,128)(2,1)} %bitcast.5, s32[8,128]{1,0:T(8,128)S(1)} %pad_add_fusion.meta, bf16[32,128,256]{2,1,0:T(8,128)(2,1)} %bitcast.4), custom_call_target="tpu_custom_call" | custom-call | flops 536870912 | bytes 4194304 | tf_op jit(solution)/shard_map/pallas_call | solution.py:306
  62.8 0.6 copy.8

commit v4 on v3

--- a/solution.py
+++ b/solution.py
@@ -14,8 +14,8 @@
 
 def kernel(dims, a_ref, meta, t_ref, out_ref,
            t_v, rxa, cmp_v, ring, meta_all, tab, tab_s, run,
-           mine, to_core, from_core, coded, from_chip,
-           loc_sem, a_send, a_recv, m_send, m_recv, g_send, g_recv, c_send, c_recv, x_send, x_recv):
+           mine, to_core, from_core, coded, from_chip, step_out, step_in,
+           loc_sem, a_send, a_recv, m_send, m_recv, g_send, g_recv, c_send, c_recv, x_send, x_recv, s_send, s_recv):
     nx, nz, ny, slots, blk, live = dims
     chips = nx * ny
     sub = blk // nz
@@ -190,14 +190,25 @@
         core_copy(t).start()
 
     def chip_copy(t, q):
-        n = 2 * rows_in(t) + sub
+        n = 2 * rows_in(t)
         x, y = on_plane(q)
         return pltpu.make_async_remote_copy(
             src_ref=coded.at[t, x * ny + y, pl.ds(0, n)], dst_ref=from_chip.at[t, q, pl.ds(0, n)],
             send_sem=x_send.at[t], recv_sem=x_recv.at[t], device_id=(x, rz, 2 * y + core), device_id_type=MESH)
 
+    def step_copy(t, q):
+        x, y = on_plane(q)
+        return pltpu.make_async_remote_copy(
+            src_ref=step_out.at[t, x * ny + y], dst_ref=step_in.at[t, q],
+            send_sem=s_send.at[t], recv_sem=s_recv.at[t], device_id=(x, rz, 2 * y + core), device_id_type=MESH)
+
+    def steps_all(t):
+        return pltpu.make_async_remote_copy(
+            src_ref=step_out.at[t, pl.ds(1, chips - 1)], dst_ref=step_in.at[t, pl.ds(1, chips - 1)],
+            send_sem=s_send.at[t], recv_sem=s_recv.at[t], device_id=other_core, device_id_type=MESH)
+
     def chips_all(t):
-        n = 2 * rows_in(t) + sub
+        n = 2 * rows_in(t)
         return pltpu.make_async_remote_copy(
             src_ref=coded.at[t, pl.ds(1, chips - 1), pl.ds(0, n)], dst_ref=from_chip.at[t, pl.ds(1, chips - 1), pl.ds(0, n)],
             send_sem=x_send.at[t], recv_sem=x_recv.at[t], device_id=other_core, device_id_type=MESH)
@@ -211,24 +222,24 @@
             value = mine[t, r, 0:n] + from_core[t, r, 0:n]
             left, right = value[:, 0:128], value[:, 128:256]
             top = jnp.max(jnp.maximum(jnp.abs(left), jnp.abs(right)), axis=0, keepdims=True)
-            power = jnp.floor(jnp.log2(jnp.maximum(top, 1e-30)) + 1.001)
-            up = jnp.exp2(15.0 - power)
+            top = jnp.maximum(top, 1e-33)
+            step_out[t, r] = top * (1.0 / 32766.0)
+            up = 32766.0 / top
             for k, half in enumerate((left, right)):
-                fixed = jnp.clip(jnp.round(half * up), -32767.0, 32767.0)
-                coded[t, r, k * n:(k + 1) * n] = fixed.astype(jnp.int32).astype(jnp.int16)
-            power = jnp.broadcast_to(power, (sub, 128))
-            coded[t, r, 2 * n:2 * n + sub] = power.astype(jnp.int32).astype(jnp.int16)
+                coded[t, r, k * n:(k + 1) * n] = jnp.round(half * up).astype(jnp.int32).astype(jnp.int16)
         for q in far_first[start:stop]:
+            step_copy(t, q).start()
             chip_copy(t, q).start()
 
     def finish(t):
         n = rows_in(t)
 
+        steps_all(t).wait_recv()
         chips_all(t).wait_recv()
 
         def add(q, acc):
-            fixed = from_chip[t, q, 0:2 * n + sub].astype(jnp.int32).astype(jnp.float32)
-            down = jnp.exp2(fixed[2 * n:2 * n + 1] - 15.0)
+            fixed = from_chip[t, q, 0:2 * n].astype(jnp.int32).astype(jnp.float32)
+            down = step_in[t, q]
             return acc[0] + fixed[0:n] * down, acc[1] + fixed[n:2 * n] * down
 
         own = mine[t, chip, 0:n] + from_core[t, chip, 0:n]
@@ -285,6 +296,7 @@
         src_ref=to_core.at[pl.ds(0, 4)], dst_ref=to_core.at[pl.ds(0, 4)], send_sem=c_send.at[0], recv_sem=c_recv.at[0],
         device_id=other_core, device_id_type=MESH).wait_send()
     for t in range(5):
+        steps_all(t).wait_send()
         chips_all(t).wait_send()
 
 
@@ -320,10 +332,12 @@
             pltpu.VMEM((5, chips, 2 * sub, width), f32),
             pltpu.VMEM((5, chips, 2 * sub, width), f32),
             pltpu.VMEM((5, chips, 2 * sub, width), f32),
-            pltpu.VMEM((5, chips, 5 * sub, 128), jnp.int16),
-            pltpu.VMEM((5, chips, 5 * sub, 128), jnp.int16),
+            pltpu.VMEM((5, chips, 4 * sub, 128), jnp.int16),
+            pltpu.VMEM((5, chips, 4 * sub, 128), jnp.int16),
+            pltpu.VMEM((5, chips, 1, 128), f32),
+            pltpu.VMEM((5, chips, 1, 128), f32),
             dma((3,)), dma((1,)), dma((1,)), dma((1,)), dma((1,)),
-            dma((1,)), dma((2, 4, CH)), dma((1,)), dma((5,)), dma((5,)), dma((5,)),
+            dma((1,)), dma((2, 4, CH)), dma((1,)), dma((5,)), dma((5,)), dma((5,)), dma((5,)), dma((5,)),
         ],
         compiler_params=pltpu.CompilerParams(
             collective_id=0, has_side_effects=True, vmem_limit_bytes=54784 * 2**10),

time: 63.5 us -> 62.5 us (0.984)
  Pallas kernels: 61.5 us -> 60.4 us
    pallas_call x1, Pallas kernels: 61.5 us -> 60.4 us  [shards(): pl.pallas_call(functools.partial(kernel, (nx, nz, ny, slots, blk, live)),...]
where the time goes in v4:
time: 62.5 us; the launch traced here: 62.4 us
  Pallas kernels  60.4 us (97%)
  other arithmetic  0.68 us (1%)
  between operations  0.66 us (1%)
  local copies, waits for them, and re-layouts  0.63 us (1%)
    pallas_call x1, Pallas kernels, shards(): pl.pallas_call(functools.partial(kernel, (nx, nz, ny, slots, blk, live)),...  60.4 us

profile of v4, /device:TPU:1, one launch (start us, length us, event | category | flops | bytes accessed | tf_op | source)
XLA Modules:
  0.0 62.4 jit_solution(11564813313053036011)
XLA Ops:
  0.7 0.7 %pad_add_fusion.meta = s32[8,128]{1,0:T(8,128)S(1)} fusion(s32[1,1]{1,0:T(1,128)S(6)} %copy.7, s32[1,24]{1,0:T(1,128)} %bitcast.6, s32[1,24]{1,0:T(1,128)} %bitcast.7), kind=kLoop, calls=%fused_computation | loop fusion | flops 2048 | bytes 4292 | tf_op jit(solution)/shard_map/concatenate | solution.py:311
  1.3 60.4 %shard_map.55 = bf16[128,256]{1,0:T(8,128)(2,1)S(1)} custom-call(bf16[24,128,128]{2,1,0:T(8,128)(2,1)} %bitcast.5, s32[8,128]{1,0:T(8,128)S(1)} %pad_add_fusion.meta, bf16[32,128,256]{2,1,0:T(8,128)(2,1)} %bitcast.4), custom_call_target="tpu_custom_call" | custom-call | flops 536870912 | bytes 4194304 | tf_op jit(solution)/shard_map/pallas_call | solution.py:318
  61.7 0.6 %copy.8 = bf16[128,256]{1,0:T(8,128)(2,1)} copy(bf16[128,256]{1,0:T(8,128)(2,1)S(1)} %shard_map.55) | data formatting | bytes 131072

commit v5 on v4

--- a/solution.py
+++ b/solution.py
@@ -52,12 +52,16 @@
 
     pl.semaphore_wait(barrier, nz - 1 + 1 + chips - 1)
 
+    near = 1
+    far_o = range(near + 1, nz - near)
+    near_o = [*range(1, near + 1), *range(nz - near, nz)]
+
     def a_copy(o):
         to = lax.rem(rz + o, nz)
         return pltpu.make_async_remote_copy(
             src_ref=a_ref.at[:, pl.ds(pl.multiple_of(to * sub, sub), sub), :],
             dst_ref=rxa.at[pl.ds(rz * slots, slots)],
-            send_sem=a_send.at[0], recv_sem=a_recv.at[0], device_id=on_z(o), device_id_type=MESH)
+            send_sem=a_send.at[0 if o in far_o else 1], recv_sem=a_recv.at[0], device_id=on_z(o), device_id_type=MESH)
 
     def m_copy(o):
         return pltpu.make_async_remote_copy(
@@ -68,12 +72,9 @@
         m_copy(o).start()
         return c_
 
-    def start_pieces(o, c_):
+    lax.fori_loop(1, nz, start_meta, 0)
+    for o in far_o:
         a_copy(o).start()
-        return c_
-
-    lax.fori_loop(1, nz, start_meta, 0)
-    lax.fori_loop(1, nz, start_pieces, 0)
     t_copy = pltpu.make_async_copy(t_ref, t_v, loc_sem.at[0])
     own_piece = pltpu.make_async_copy(
         a_ref.at[:, pl.ds(pl.multiple_of(rz * sub, sub), sub), :], rxa.at[pl.ds(rz * slots, slots)], loc_sem.at[1])
@@ -127,6 +128,13 @@
     table = pltpu.make_async_copy(tab, tab_s, loc_sem.at[2])
     table.start()
     run[live] = jnp.zeros(run.shape[1:], jnp.float32)
+    a_sent = [pltpu.make_async_remote_copy(
+        src_ref=rxa.at[pl.ds(0, k * slots)], dst_ref=rxa.at[pl.ds(0, k * slots)],
+        send_sem=a_send.at[i], recv_sem=a_recv.at[0], device_id=other_core, device_id_type=MESH)
+        for i, k in enumerate((len(far_o), len(near_o)))]
+    a_sent[0].wait_send()
+    for o in near_o:
+        a_copy(o).start()
     table.wait()
     t_copy.wait()
     own_piece.wait()
@@ -288,7 +296,7 @@
     finish(4)
 
     m_all.wait_send()
-    a_all.wait_send()
+    a_sent[1].wait_send()
     pltpu.make_async_remote_copy(
         src_ref=ring, dst_ref=ring, send_sem=g_send.at[0], recv_sem=g_recv.at[0, 0, 0],
         device_id=other_core, device_id_type=MESH).wait_send()
@@ -336,7 +344,7 @@
             pltpu.VMEM((5, chips, 4 * sub, 128), jnp.int16),
             pltpu.VMEM((5, chips, 1, 128), f32),
             pltpu.VMEM((5, chips, 1, 128), f32),
-            dma((3,)), dma((1,)), dma((1,)), dma((1,)), dma((1,)),
+            dma((3,)), dma((2,)), dma((1,)), dma((1,)), dma((1,)),
             dma((1,)), dma((2, 4, CH)), dma((1,)), dma((5,)), dma((5,)), dma((5,)), dma((5,)), dma((5,)),
         ],
         compiler_params=pltpu.CompilerParams(

time: 62.5 us -> 61.9 us (level)
  no operation moved by 1% of the time
where the time goes in v5:
time: 61.9 us; the launch traced here: 61.8 us
  Pallas kernels  59.8 us (97%)
  other arithmetic  0.68 us (1%)
  between operations  0.66 us (1%)
  local copies, waits for them, and re-layouts  0.63 us (1%)
    pallas_call x1, Pallas kernels, shards(): pl.pallas_call(functools.partial(kernel, (nx, nz, ny, slots, blk, live)),...  59.8 us

profile of v5, /device:TPU:1, one launch (start us, length us, event | category | flops | bytes accessed | tf_op | source)
XLA Modules:
  0.0 61.8 jit_solution(4458087205892771267)
XLA Ops:
  0.7 0.7 %pad_add_fusion.meta = s32[8,128]{1,0:T(8,128)S(1)} fusion(s32[1,1]{1,0:T(1,128)S(6)} %copy.7, s32[1,24]{1,0:T(1,128)} %bitcast.6, s32[1,24]{1,0:T(1,128)} %bitcast.7), kind=kLoop, calls=%fused_computation | loop fusion | flops 2048 | bytes 4292 | tf_op jit(solution)/shard_map/concatenate | solution.py:319
  1.3 59.8 %shard_map.55 = bf16[128,256]{1,0:T(8,128)(2,1)S(1)} custom-call(bf16[24,128,128]{2,1,0:T(8,128)(2,1)} %bitcast.5, s32[8,128]{1,0:T(8,128)S(1)} %pad_add_fusion.meta, bf16[32,128,256]{2,1,0:T(8,128)(2,1)} %bitcast.4), custom_call_target="tpu_custom_call" | custom-call | flops 536870912 | bytes 4194304 | tf_op jit(solution)/shard_map/pallas_call | solution.py:326
  61.1 0.6 %copy.8 = bf16[128,256]{1,0:T(8,128)(2,1)} copy(bf16[128,256]{1,0:T(8,128)(2,1)S(1)} %shard_map.55) | data formatting | bytes 131072
